TPU v7x, 512 devices: a whole 4x4x16 slice. The times are simulated.
512 devices in a mesh: snd: 32 (over y, x, core), rcv: 16 (over z).
Axes of the slice: x: 4, y: 4, z: 16, core: 2. Of those that a mesh axis runs over, the one named last changes fastest.
Arguments:
- nodes: bfloat16 [4096, 512], P(('snd', 'rcv')), may hold values from -6 to 6
- edges: bfloat16 [32, 16, 256, 512], P('snd', 'rcv'), may hold values from -6 to 6
- send_local: int32 [32, 16, 256], P('snd', 'rcv'), may hold values from 0 to 127
- recv_local: int32 [32, 16, 256], P('snd', 'rcv'), may hold values from 0 to 255
- edge_count: int32 [32, 16], P('snd', 'rcv'), may hold values from 32 to 256, as said below
- edge_w1: bfloat16 [1536, 512], replicated, may hold values from -0.15625 to 0.15625
- edge_w2: bfloat16 [512, 512], replicated, may hold values from -0.25 to 0.25
- node_w1: bfloat16 [1024, 512], replicated, may hold values from -0.1875 to 0.1875
- node_w2: bfloat16 [512, 512], replicated, may hold values from -0.25 to 0.25
- grad_nodes_out: bfloat16 [4096, 512], P(('snd', 'rcv')), may hold values from -6 to 6
- grad_edges_out: bfloat16 [32, 16, 256, 512], P('snd', 'rcv'), may hold values from -6 to 6
Outputs:
- grad_nodes: float32 [4096, 512], P(('snd', 'rcv'))
- grad_edges: float32 [32, 16, 256, 512], P('snd', 'rcv')
Inputs may be any that keep to these rules, and one draw needn't show every extreme that they name: Live edges of a tile fill its first edge_count slots; in every draw some tile has all 256 slots live.
All inputs are finite; a program needn't handle non-finite values.
Results may differ from a plain program's by a relative error of at most 0.019.
Values may be sent and summed in bfloat16 or wider, within the bound.
A program may use at most 64 MiB of HBM per device.

v0:
```python
import jax
import jax.numpy as jnp
from jax import lax
from jax.sharding import PartitionSpec as P


def swish_slope(pre_act):
    sigma = jax.nn.sigmoid(pre_act)
    return sigma * (1.0 + pre_act * (1.0 - sigma))


def layer_norm(values):
    center = values - jnp.mean(values, -1, keepdims=True)
    inv_scale = lax.rsqrt(jnp.mean(center * center, -1, keepdims=True) + 1e-05)
    return (center * inv_scale, inv_scale)


def norm_backward(upstream, normed, inv_scale):
    return inv_scale * (
        upstream
        - jnp.mean(upstream, -1, keepdims=True)
        - normed * jnp.mean(upstream * normed, -1, keepdims=True)
    )


def mlp_forward(inputs_cat, first_w, second_w):
    pre_act = jnp.dot(inputs_cat, first_w, preferred_element_type=jnp.float32)
    hidden = jax.nn.silu(pre_act).astype(jnp.bfloat16)
    output = jnp.dot(hidden, second_w, preferred_element_type=jnp.float32)
    normed, inv_scale = layer_norm(output)
    return (pre_act, normed, inv_scale)


def mlp_backward(upstream, pre_act, normed, inv_scale, first_w, second_w):
    grad_out = norm_backward(upstream, normed, inv_scale).astype(jnp.bfloat16)
    grad_hidden = jnp.dot(grad_out, second_w.T, preferred_element_type=jnp.float32)
    grad_pre = (grad_hidden * swish_slope(pre_act)).astype(jnp.bfloat16)
    return jnp.dot(grad_pre, first_w.T, preferred_element_type=jnp.float32)


def node_backward(node_feat, aggregate, upstream_bf, node_w1, node_w2):
    feat_width = node_feat.shape[1]
    inputs_cat = jnp.concatenate([node_feat, aggregate.astype(jnp.bfloat16)], 1)
    pre_act, normed, inv_scale = mlp_forward(inputs_cat, node_w1, node_w2)
    upstream = upstream_bf.astype(jnp.float32)
    grad_in = mlp_backward(upstream, pre_act, normed, inv_scale, node_w1, node_w2)
    return (upstream + grad_in[:, :feat_width], grad_in[:, feat_width:])


def select_cols(indices, offset, span_rows, dtype):
    columns = jnp.arange(span_rows, dtype=jnp.int32)[None, :]
    return (indices[:, None] - offset == columns).astype(dtype)


def fold_bf16(indices, shard_rows, offset):
    picker = select_cols(indices, offset, shard_rows.shape[0], jnp.bfloat16)
    return jnp.dot(picker, shard_rows, preferred_element_type=jnp.float32)


def scatter_term(indices, values, offset, span_rows):
    picker = select_cols(indices, offset, span_rows, jnp.float32)
    return jnp.dot(picker.T, values, precision=lax.Precision.HIGHEST)


def local(
    nodes,
    edges,
    send_local,
    recv_local,
    edge_count,
    edge_w1,
    edge_w2,
    node_w1,
    node_w2,
    grad_nodes_out,
    grad_edges_out,
):
    node_rows = nodes.shape[0]
    edge_slots = edges.shape[2]
    feat_width = edges.shape[3]
    edge_feat = edges[0, 0]
    send_idx = send_local[0, 0]
    recv_idx = recv_local[0, 0]
    live_mask = (jnp.arange(edge_slots, dtype=jnp.int32) < edge_count[0, 0]).astype(jnp.float32)[
        :, None
    ]
    sender_edge = fold_bf16(
        send_idx, lax.all_gather(nodes, "rcv", axis=0, tiled=True), jnp.int32(0)
    ).astype(jnp.bfloat16)
    group_nodes, group_upstream = (
        lax.all_gather(nodes, "snd", axis=0, tiled=True),
        lax.all_gather(grad_nodes_out, "snd", axis=0, tiled=True),
    )
    picker = select_cols(recv_idx, 0, group_nodes.shape[0], jnp.bfloat16)
    receiver_edge = jnp.dot(picker, group_nodes, preferred_element_type=jnp.float32).astype(
        jnp.bfloat16
    )
    inputs_cat = jnp.concatenate([edge_feat, sender_edge, receiver_edge], 1)
    pre_act, normed, inv_scale = mlp_forward(inputs_cat, edge_w1, edge_w2)
    picker_f32 = picker.astype(jnp.float32)
    partial_agg = jnp.dot(picker_f32.T, normed * live_mask, precision=lax.Precision.HIGHEST)
    aggregate = lax.psum(partial_agg.astype(jnp.bfloat16), "snd").astype(jnp.float32)
    direct_all, agg_grad_all = node_backward(
        group_nodes, aggregate, group_upstream, node_w1, node_w2
    )
    direct = lax.dynamic_slice_in_dim(direct_all, lax.axis_index("snd") * node_rows, node_rows, 0)
    agg_grad_edge = jnp.dot(picker_f32, agg_grad_all, precision=lax.Precision.HIGHEST)
    cotangent = grad_edges_out[0, 0].astype(jnp.float32)
    upstream = (cotangent + agg_grad_edge) * live_mask
    grad_in = mlp_backward(upstream, pre_act, normed, inv_scale, edge_w1, edge_w2)
    edge_grad = live_mask * cotangent + grad_in[:, :feat_width]
    send_part = grad_in[:, feat_width : 2 * feat_width]
    recv_part = grad_in[:, 2 * feat_width :]
    send_own = lax.psum_scatter(
        scatter_term(send_idx, send_part, jnp.int32(0), node_rows * lax.axis_size("rcv")).astype(
            jnp.bfloat16
        ),
        "rcv",
        scatter_dimension=0,
        tiled=True,
    ).astype(jnp.float32)
    recv_own = lax.psum_scatter(
        scatter_term(recv_idx, recv_part, jnp.int32(0), node_rows * lax.axis_size("snd")).astype(
            jnp.bfloat16
        ),
        "snd",
        scatter_dimension=0,
        tiled=True,
    ).astype(jnp.float32)
    return (direct + send_own + recv_own, edge_grad[None, None])


def solution(mesh):
    in_specs = (
        P(("snd", "rcv"), None),
        P("snd", "rcv", None, None),
        P("snd", "rcv", None),
        P("snd", "rcv", None),
        P("snd", "rcv"),
        P(),
        P(),
        P(),
        P(),
        P(("snd", "rcv"), None),
        P("snd", "rcv", None, None),
    )
    out_specs = (P(("snd", "rcv"), None), P("snd", "rcv", None, None))
    return jax.shard_map(local, mesh=mesh, in_specs=in_specs, out_specs=out_specs, check_vma=False)
```

profile of v0, /device:TPU:2, one launch (start us, length us, event | category | flops | bytes accessed | tf_op | source)
XLA Modules:
  0.0 394.0 jit_solution(5266284681063897507)
XLA Ops:
  7.2 0.0 copy-start
  7.2 0.0 all-reduce.2.cloned.1.call-start
  7.2 36.5 %all_gather.11 = bf16[128,512]{1,0:T(8,128)(2,1)S(1)} all-gather(bf16[8,512]{1,0:T(8,128)(2,1)} %param.11), channel_id=1, replica_groups=mesh['snd'=32,'rcv'=16] {'rcv'}, dimensions={0}, use_global_device_ids=true | all-gather | bytes 139264 | tf_op jit(solution)/shard_map/all_gather | solution.py:88
  43.7 24.8 %all_gather.10 = bf16[256,512]{1,0:T(8,128)(2,1)S(1)} all-gather(bf16[8,512]{1,0:T(8,128)(2,1)} %param.11), channel_id=1, replica_groups=mesh['snd'=32,'rcv'=16] {'snd'}, dimensions={0}, use_global_device_ids=true | all-gather | bytes 270336 | tf_op jit(solution)/shard_map/all_gather | solution.py:91
  69.1 0.9 convolution_convert_fusion.3
  70.1 1.0 convolution_convert_fusion.2
  71.0 0.0 copy-done
  71.0 0.0 copy-start.5
  71.1 1.6 fusion.5
  72.6 0.0 copy-done.5
  72.6 0.0 copy-start.7
  72.7 0.0 copy-start.2
  72.7 0.0 copy-start.3
  72.7 0.4 fusion.69
  73.1 0.2 multiply_reduce_fusion.3
  73.3 0.1 copy-done.7
  73.5 0.0 copy-done.2
  73.5 1.3 convolution_convert_fusion.1
  74.8 0.0 all-reduce.2.cloned.1.call-update
  74.8 0.0 reduce-scatter.3.cloned.1.call-start
  74.8 0.0 copy-done.3
  74.8 23.1 %all_gather.9 = bf16[256,512]{1,0:T(8,128)(2,1)S(1)} all-gather(bf16[8,512]{1,0:T(8,128)(2,1)S(1)} %copy-done.3), channel_id=1, replica_groups=mesh['snd'=32,'rcv'=16] {'snd'}, dimensions={0}, use_global_device_ids=true | all-gather | bytes 270336 | tf_op jit(solution)/shard_map/all_gather | solution.py:92
  97.9 102.9 %all-reduce.2.cloned.1.call-done = bf16[256,512]{1,0:T(8,128)(2,1)} async-done(((bf16[256,512]{1,0:T(8,128)(2,1)}), bf16[256,512]{1,0:T(8,128)(2,1)}) %all-reduce.2.cloned.1.call-update) | async-done | bytes 262160 | tf_op jit(solution)/shard_map/psum | solution.py:102
  200.8 1.7 fusion.16
  202.6 0.0 copy-start.6
  202.6 1.6 fusion.70
  204.3 0.2 multiply_reduce_fusion.2
  204.5 0.0 copy-done.6
  204.5 0.2 convert_reduce_fusion
  204.8 0.0 copy-start.1
  204.8 3.4 fusion.4
  208.1 0.0 copy-done.1
  208.1 1.7 fusion.68
  209.9 0.0 copy-start.4
  209.9 3.3 fusion.3
  213.2 0.0 copy-done.4
  213.2 2.1 convolution_convert_fusion.4
  215.2 0.0 reduce-scatter.3.cloned.1.call-update
  215.3 0.0 reduce-scatter.5.cloned.1.call-start
  215.3 2.3 convolution_convert_fusion
  217.6 0.0 reduce-scatter.5.cloned.1.call-update
  217.6 0.0 slice-start
  217.6 0.1 convert_element_type.62
  217.7 2.0 fusion.12
  219.7 64.6 %reduce-scatter.3.cloned.1.call-done = bf16[8,512]{1,0:T(8,128)(2,1)} async-done(((bf16[128,512]{1,0:T(8,128)(2,1)}), bf16[8,512]{1,0:T(8,128)(2,1)}) %reduce-scatter.3.cloned.1.call-update) | async-done | bytes 8208 | tf_op jit(solution)/shard_map/reduce_scatter | solution.py:114
  284.2 102.0 %reduce-scatter.5.cloned.1.call-done = bf16[8,512]{1,0:T(8,128)(2,1)} async-done(((bf16[256,512]{1,0:T(8,128)(2,1)}), bf16[8,512]{1,0:T(8,128)(2,1)}) %reduce-scatter.5.cloned.1.call-update) | async-done | bytes 8208 | tf_op jit(solution)/shard_map/reduce_scatter | solution.py:122
  386.2 0.0 slice-done
  386.2 1.3 fusion.61
  (8 shorter events, 0.0 us)
Async XLA Ops:
  7.2 63.9 %copy-start = (bf16[1536,512]{1,0:T(8,128)(2,1)S(1)}, bf16[1536,512]{1,0:T(8,128)(2,1)}, u32[]{:S(2)}) copy-start(bf16[1536,512]{1,0:T(8,128)(2,1)} %param.16) | copy-start | bytes 4718596
  7.2 193.7 %all-reduce.2.cloned.1.call-start = ((), (), s32[]{:S(2)}) async-start(), calls=%async_computation.2 | async-start | bytes 524288 | tf_op jit(solution)/shard_map/psum | solution.py:102
  71.0 1.6 copy-start.5
  72.6 0.8 copy-start.7
  72.7 0.8 copy-start.2
  72.7 2.2 copy-start.3
  74.8 209.4 %reduce-scatter.3.cloned.1.call-start = ((), (), s32[]{:S(2)}) async-start(), calls=%async_computation.3 | async-start | bytes 139264 | tf_op jit(solution)/shard_map/reduce_scatter | solution.py:114
  202.6 1.9 copy-start.6
  204.8 3.4 copy-start.1
  209.9 3.3 copy-start.4
  215.3 170.9 %reduce-scatter.5.cloned.1.call-start = ((), (), s32[]{:S(2)}) async-start(), calls=%async_computation.4 | async-start | bytes 270336 | tf_op jit(solution)/shard_map/reduce_scatter | solution.py:122
  217.6 168.6 %slice-start = ((f32[256,1024]{1,0:T(8,128)}), f32[256,512]{1,0:T(8,128)S(1)}, s32[]{:S(2)}) async-start(f32[256,1024]{1,0:T(8,128)} %fusion.4), calls=%async_computation.5 | async-start | bytes 1048576 | tf_op jit(solution)/shard_map/slice | solution.py:47
Sparse Core Ops, SparseCore 0:
  74.9 125.8 all-reduce.1
  215.4 68.7 reduce-scatter.2
  288.5 97.5 reduce-scatter.4
where the time goes:
time: 395 us; the launch traced here: 394 us
  waiting for transfers between devices  269 us (68%)
  blocking collectives  84.3 us (21%)
  matrix products  21.2 us (5%)
  between operations  14.6 us (4%)
  other arithmetic  4.08 us (1%)
    psum x1, waiting for transfers between devices, local(): lax.psum(partial_agg.astype(jnp.bfloat16), 'snd').astype(jnp.float32)  103 us
    reduce_scatter x1, waiting for transfers between devices, local(): lax.psum_scatter(scatter_term(recv_idx, recv_part, jnp.int32(0), node_row...  102 us
    reduce_scatter x1, waiting for transfers between devices, local(): lax.psum_scatter(scatter_term(send_idx, send_part, jnp.int32(0), node_row...  64.6 us
    all_gather x1, blocking collectives, local(): lax.all_gather(nodes, 'rcv', axis=0, tiled=True)  36.5 us
    all_gather x1, blocking collectives, local(): lax.all_gather(nodes, 'snd', axis=0, tiled=True)  24.8 us
    all_gather x1, blocking collectives, local(): lax.all_gather(grad_nodes_out, 'snd', axis=0, tiled=True)  23.1 us
  transfers between devices with their start and end apart: 3, of which 3 were waited for; matrix products, arithmetic and copies ran while one was open for 1% of the time, Pallas kernels for 0%

commit v1 on v0

--- a/solution.py
+++ b/solution.py
@@ -99,7 +99,9 @@
     pre_act, normed, inv_scale = mlp_forward(inputs_cat, edge_w1, edge_w2)
     picker_f32 = picker.astype(jnp.float32)
     partial_agg = jnp.dot(picker_f32.T, normed * live_mask, precision=lax.Precision.HIGHEST)
-    aggregate = lax.psum(partial_agg.astype(jnp.bfloat16), "snd").astype(jnp.float32)
+    aggregate = jnp.sum(lax.all_gather(partial_agg.astype(jnp.bfloat16), "snd"), axis=0).astype(
+        jnp.float32
+    )
     direct_all, agg_grad_all = node_backward(
         group_nodes, aggregate, group_upstream, node_w1, node_w2
     )

time: 395 us -> 335 us (0.85)
  waiting for transfers between devices: 269 us -> 206 us
  other arithmetic: 4.08 us -> 8.84 us
    psum x1 -> x0, waiting for transfers between devices: 103 us -> none  [local(): lax.psum(partial_agg.astype(jnp.bfloat16), 'snd').astype(jnp.float32)]
    all_gather x0 -> x1, waiting for transfers between devices: none -> 39.5 us  [local(): lax.all_gather(partial_agg.astype(jnp.bfloat16), 'snd')]
    reduce_sum x0 -> x1, other arithmetic: none -> 4.75 us  [local(): jnp.sum(lax.all_gather(partial_agg.astype(jnp.bfloat16), 'snd'), axis=0)]
where the time goes in v1:
time: 335 us; the launch traced here: 334 us
  waiting for transfers between devices  206 us (61%)
  blocking collectives  84.4 us (25%)
  matrix products  20 us (6%)
  between operations  14.6 us (4%)
  other arithmetic  8.84 us (3%)
    reduce_scatter x1, waiting for transfers between devices, local(): lax.psum_scatter(scatter_term(recv_idx, recv_part, jnp.int32(0), node_row...  102 us
    reduce_scatter x1, waiting for transfers between devices, local(): lax.psum_scatter(scatter_term(send_idx, send_part, jnp.int32(0), node_row...  64 us
    all_gather x1, waiting for transfers between devices, local(): lax.all_gather(partial_agg.astype(jnp.bfloat16), 'snd')  39.5 us
    all_gather x1, blocking collectives, local(): lax.all_gather(nodes, 'rcv', axis=0, tiled=True)  33.5 us
    all_gather x1, blocking collectives, local(): lax.all_gather(nodes, 'snd', axis=0, tiled=True)  27.8 us
    all_gather x1, blocking collectives, local(): lax.all_gather(grad_nodes_out, 'snd', axis=0, tiled=True)  23.1 us
  transfers between devices with their start and end apart: 3, of which 3 were waited for; matrix products, arithmetic and copies ran while one was open for 1% of the time, Pallas kernels for 0%

profile of v1, /device:TPU:2, one launch (start us, length us, event | category | flops | bytes accessed | tf_op | source)
XLA Modules:
  0.0 334.1 jit_solution(927026904238378874)
XLA Ops:
  7.2 0.0 copy-start
  7.2 0.0 all-gather.3.cloned.1.call-start
  7.2 27.8 %all_gather.16 = bf16[256,512]{1,0:T(8,128)(2,1)S(1)} all-gather(bf16[8,512]{1,0:T(8,128)(2,1)} %param.11), channel_id=1, replica_groups=mesh['snd'=32,'rcv'=16] {'snd'}, dimensions={0}, use_global_device_ids=true | all-gather | bytes 270336 | tf_op jit(solution)/shard_map/all_gather | solution.py:91
  35.0 33.5 %all_gather.17 = bf16[128,512]{1,0:T(8,128)(2,1)S(1)} all-gather(bf16[8,512]{1,0:T(8,128)(2,1)} %param.11), channel_id=1, replica_groups=mesh['snd'=32,'rcv'=16] {'rcv'}, dimensions={0}, use_global_device_ids=true | all-gather | bytes 139264 | tf_op jit(solution)/shard_map/all_gather | solution.py:88
  68.5 0.9 convolution_convert_fusion.2
  69.4 0.9 convolution_convert_fusion.3
  70.4 0.0 copy-done
  70.4 0.0 copy-start.6
  70.4 1.6 fusion.5
  72.0 0.0 copy-done.6
  72.0 0.0 copy-start.8
  72.0 0.0 copy-start.2
  72.0 0.0 copy-start.3
  72.0 0.4 fusion.69
  72.5 0.2 multiply_reduce_fusion.3
  72.7 0.2 copy-done.8
  73.5 0.0 copy-done.2
  73.5 1.3 convolution_convert_fusion.1
  74.8 0.0 all-gather.3.cloned.1.call-update
  74.8 0.0 reduce-scatter.3.cloned.1.call-start
  74.9 0.0 copy-done.3
  74.9 23.1 %all_gather.15 = bf16[256,512]{1,0:T(8,128)(2,1)S(1)} all-gather(bf16[8,512]{1,0:T(8,128)(2,1)S(1)} %copy-done.3), channel_id=1, replica_groups=mesh['snd'=32,'rcv'=16] {'snd'}, dimensions={0}, use_global_device_ids=true | all-gather | bytes 270336 | tf_op jit(solution)/shard_map/all_gather | solution.py:92
  98.0 39.5 %all-gather.3.cloned.1.call-done = bf16[8192,512]{1,0:T(8,128)(2,1)} async-done(((bf16[256,512]{1,0:T(8,128)(2,1)}), bf16[8192,512]{1,0:T(8,128)(2,1)}) %all-gather.3.cloned.1.call-update) | async-done | bytes 8388624 | tf_op jit(solution)/shard_map/all_gather | solution.py:102
  137.5 4.8 %reduce_sum.86 = bf16[256,512]{1,0:T(8,128)(2,1)S(1)} reduce(bf16[32,256,512]{2,1,0:T(8,128)(2,1)} %bitcast.22, bf16[]{:T(256)} %constant.27.clone.1), dimensions={0}, to_apply=%region_2.3 | reduce | flops 4063232 | bytes 8650754 | tf_op jit(solution)/shard_map/reduce_sum | solution.py:102
  142.2 0.0 copy-start.5
  142.3 1.7 fusion.16
  144.0 0.0 copy-done.5
  144.0 0.0 copy-start.7
  144.0 0.4 fusion.70
  144.4 0.2 multiply_reduce_fusion.2
  144.6 0.2 copy-done.7
  144.8 0.3 convert_reduce_fusion
  145.1 0.0 copy-start.1
  145.1 3.4 %fusion.4 = f32[256,1024]{1,0:T(8,128)} fusion(bf16[1024,512]{1,0:T(8,128)(2,1)} %param.18, bf16[512,512]{1,0:T(8,128)(2,1)} %param.19, f32[256,512]{1,0:T(8,128)} %copy-done.7, f32[256,512]{1,0:T(8,128)S(1)} %get-tuple-element.9, bf16[256,512]{1,0:T(8,128)(2,1)S(1)} %all_gather.15, f32[256]{0:T(256)S(1)} %get-tuple-element.11, ...), kind=kOutput, calls=%fused_computation.11 | convolution fusion | flops 404881408 | bytes 3936256 | tf_op jit(solution)/shard_map/dot_general | solution.py:38
  148.4 0.0 copy-done.1
  148.4 1.7 fusion.68
  150.1 0.0 copy-start.4
  150.2 3.3 fusion.3
  153.5 0.0 copy-done.4
  153.5 2.1 convolution_convert_fusion.4
  155.5 0.0 reduce-scatter.3.cloned.1.call-update
  155.6 0.0 reduce-scatter.5.cloned.1.call-start
  155.6 2.3 convolution_convert_fusion
  157.9 0.0 reduce-scatter.5.cloned.1.call-update
  157.9 0.0 slice-start
  157.9 0.1 convert_element_type.64
  158.0 2.0 fusion.12
  160.0 64.0 %reduce-scatter.3.cloned.1.call-done = bf16[8,512]{1,0:T(8,128)(2,1)} async-done(((bf16[128,512]{1,0:T(8,128)(2,1)}), bf16[8,512]{1,0:T(8,128)(2,1)}) %reduce-scatter.3.cloned.1.call-update) | async-done | bytes 8208 | tf_op jit(solution)/shard_map/reduce_scatter | solution.py:116
  223.9 102.3 %reduce-scatter.5.cloned.1.call-done = bf16[8,512]{1,0:T(8,128)(2,1)} async-done(((bf16[256,512]{1,0:T(8,128)(2,1)}), bf16[8,512]{1,0:T(8,128)(2,1)}) %reduce-scatter.5.cloned.1.call-update) | async-done | bytes 8208 | tf_op jit(solution)/shard_map/reduce_scatter | solution.py:124
  326.3 0.0 slice-done
  326.3 1.3 fusion.61
  (8 shorter events, 0.0 us)
Async XLA Ops:
  7.2 63.2 %copy-start = (bf16[1536,512]{1,0:T(8,128)(2,1)S(1)}, bf16[1536,512]{1,0:T(8,128)(2,1)}, u32[]{:S(2)}) copy-start(bf16[1536,512]{1,0:T(8,128)(2,1)} %param.16) | copy-start | bytes 4718596
  7.2 130.3 %all-gather.3.cloned.1.call-start = ((), (), s32[]{:S(2)}) async-start(), calls=%async_computation.4 | async-start | bytes 8650752 | tf_op jit(solution)/shard_map/all_gather | solution.py:102
  70.4 1.6 copy-start.6
  72.0 0.8 copy-start.8
  72.0 1.5 copy-start.2
  72.0 2.9 copy-start.3
  74.8 149.1 %reduce-scatter.3.cloned.1.call-start = ((), (), s32[]{:S(2)}) async-start(), calls=%async_computation.2 | async-start | bytes 139264 | tf_op jit(solution)/shard_map/reduce_scatter | solution.py:116
  142.2 1.7 copy-start.5
  144.0 0.8 copy-start.7
  145.1 3.4 %copy-start.1 = (bf16[1,1,256,512]{3,2,1,0:T(8,128)(2,1)S(1)}, bf16[1,1,256,512]{3,2,1,0:T(8,128)(2,1)}, u32[]{:S(2)}) copy-start(bf16[1,1,256,512]{3,2,1,0:T(8,128)(2,1)} %param.21) | copy-start | bytes 786436
  150.1 3.3 copy-start.4
  155.6 170.7 %reduce-scatter.5.cloned.1.call-start = ((), (), s32[]{:S(2)}) async-start(), calls=%async_computation.3 | async-start | bytes 270336 | tf_op jit(solution)/shard_map/reduce_scatter | solution.py:124
  157.9 168.4 %slice-start = ((f32[256,1024]{1,0:T(8,128)}), f32[256,512]{1,0:T(8,128)S(1)}, s32[]{:S(2)}) async-start(f32[256,1024]{1,0:T(8,128)} %fusion.4), calls=%async_computation.5 | async-start | bytes 1048576 | tf_op jit(solution)/shard_map/slice | solution.py:47
Sparse Core Ops, SparseCore 0:
  75.0 62.4 all-gather.2
  155.7 68.2 reduce-scatter.2
  228.9 97.3 reduce-scatter.4
